TPU v7x, 256 devices: a whole 4x4x8 slice. The times are simulated.
256 devices in a mesh: expert: 8 (over z), dp: 32 (over y, x, core).
Axes of the slice: x: 4, y: 4, z: 8, core: 2. Of those that a mesh axis runs over, the one named last changes fastest.
Arguments:
- grads: bfloat16 [32, 3, 768, 2048], P('expert', None, 'dp'), may hold values from -5000 to 5000
- momentum: bfloat16 [32, 3, 768, 2048], P('expert', None, 'dp'), may hold values from -50 to 50
Outputs:
- new_momentum: bfloat16 [32, 3, 768, 2048], P('expert', None, 'dp')
- update: bfloat16 [32, 3, 768, 2048], P('expert', None, 'dp')
All inputs are finite; a program needn't handle non-finite values.
Results may differ from a plain program's by a relative error of at most 0.015.
Values may be sent and summed in bfloat16 or wider, within the bound.
A program may use at most 64 MiB of HBM per device.

v0:
```python
import math

import jax
import jax.numpy as jnp
from jax import lax
from jax.sharding import PartitionSpec as P

ITERS = 2


lin_coef = 3.4445
cub_coef = -4.775
quint_coef = 2.0315
epsilon = 1e-07
momentum_rate = 0.95


def newton_step(own_rows, full, gram_full, own_gram):
    square = jnp.einsum("kfg,kgh->kfh", own_gram, gram_full, preferred_element_type=jnp.float32)
    mix = (cub_coef * own_gram.astype(jnp.float32) + quint_coef * square).astype(jnp.bfloat16)
    product = jnp.einsum("kfg,kgd->kfd", mix, full, preferred_element_type=jnp.float32)
    return (lin_coef * own_rows.astype(jnp.float32) + product).astype(jnp.bfloat16)


def orthogonalize(stacked):
    wide = stacked.astype(jnp.float32)
    norm_value = jnp.sqrt(jnp.sum(wide * wide, axis=(1, 2))) + epsilon
    iterate = (wide / norm_value[:, None, None]).astype(jnp.bfloat16)
    for step in range(ITERS):
        gram = jnp.einsum(
            "kfd,kgd->kfg", iterate, iterate, preferred_element_type=jnp.float32
        ).astype(jnp.bfloat16)
        iterate = newton_step(iterate, iterate, gram, gram)
    return iterate


def shards(grads, momentum):
    count_dp = lax.axis_size("dp")
    groups, three, shard_rows, width = grads.shape
    total_rows = shard_rows * count_dp
    matrices = groups * three
    wide_grads = grads.astype(jnp.float32)
    total = lax.psum(jnp.sum(wide_grads * wide_grads), ("expert", "dp"))
    count = matrices * shard_rows * width * count_dp * lax.axis_size("expert")
    clip = 1.0 / jnp.maximum(jnp.sqrt(total / count), 1.0)
    moment = momentum_rate * momentum.astype(jnp.float32) + clip * wide_grads
    lead = (clip * wide_grads + momentum_rate * moment).astype(jnp.bfloat16)
    flat = lead.reshape(matrices, shard_rows, width)
    slots = -(-matrices // count_dp)
    filler = jnp.zeros((slots * count_dp - matrices, shard_rows, width), jnp.bfloat16)
    sending = jnp.concatenate([flat, filler], axis=0).reshape(slots, count_dp, shard_rows, width)
    block = lax.all_to_all(sending, "dp", split_axis=1, concat_axis=1, tiled=True)
    items = block.shape[0]
    ortho = orthogonalize(block.reshape(items, total_rows, width))
    returned = lax.all_to_all(
        ortho.reshape(items, count_dp, shard_rows, width),
        "dp",
        split_axis=1,
        concat_axis=1,
        tiled=True,
    )
    result = returned.reshape(slots * count_dp, shard_rows, width)[:matrices]
    scale_value = 0.2 * math.sqrt(max(total_rows, width))
    update = (scale_value * result.astype(jnp.float32)).astype(jnp.bfloat16).reshape(grads.shape)
    return (moment.astype(jnp.bfloat16), update)


def solution(mesh):
    placed = (P("expert", None, "dp", None), P("expert", None, "dp", None))
    return jax.shard_map(
        shards,
        mesh=mesh,
        in_specs=placed,
        out_specs=(P("expert", None, "dp", None), P("expert", None, "dp", None)),
        check_vma=False,
    )
```

profile of v0, /device:TPU:1, one launch (start us, length us, event | category | flops | bytes accessed | tf_op | source)
XLA Modules:
  0.0 206.1 jit_solution(9140712475989349754)
XLA Ops:
  0.6 2.5 %fusion.5 = f32[]{:T(128)} fusion(bf16[4,3,24,2048]{3,2,1,0:T(8,128)(2,1)} %param.2), kind=kLoop, calls=%fused_computation.12 | loop fusion | flops 1769471 | bytes 1179652 | tf_op jit(solution)/shard_map/reduce_sum | solution.py:43
  3.1 81.4 %psum.7 = f32[]{:T(128)} all-reduce(f32[]{:T(128)} %fusion.5), channel_id=1, replica_groups=mesh['expert'=8,'dp'=32] {'expert','dp'}, use_global_device_ids=true, to_apply=%region_1.0 | all-reduce | flops 1 | bytes 8 | tf_op jit(solution)/shard_map/psum | solution.py:43
  85.2 3.3 %fusion.4 = (bf16[4,3,24,2048]{3,2,1,0:T(8,128)(2,1)S(1)}, bf16[4,3,24,2048]{3,2,1,0:T(8,128)(2,1)}) fusion(bf16[4,3,24,2048]{3,2,1,0:T(8,128)(2,1)} %param.2, bf16[4,3,24,2048]{3,2,1,0:T(8,128)(2,1)} %param.3, f32[]{:T(128)S(6)} %div.24), kind=kLoop, calls=%fused_computation.11 | loop fusion | flops 5308416 | bytes 4718596 | tf_op jit(solution)/shard_map/convert_element_type | solution.py:47
  88.5 0.4 pad_bitcast_fusion
  88.9 43.6 %all_to_all.10 = bf16[1,32,24,2048]{3,2,0,1:T(8,128)(2,1)S(1)} all-to-all(bf16[1,32,24,2048]{3,2,0,1:T(8,128)(2,1)S(1)} %pad_bitcast_fusion), channel_id=1, replica_groups=mesh['expert'=8,'dp'=32] {'dp'}, dimensions={1} | all-to-all | bytes 6291456 | tf_op jit(solution)/shard_map/all_to_all | solution.py:52
  132.5 2.2 %fusion = f32[]{:T(128)} fusion(bf16[1,32,24,2048]{3,2,0,1:T(8,128)(2,1)S(1)} %all_to_all.10), kind=kLoop, calls=%fused_computation.2 | loop fusion | flops 4718591 | bytes 3145732 | tf_op jit(solution)/shard_map/reduce_sum | solution.py:27
  135.4 0.7 fusion.1
  136.1 0.0 copy-start
  136.1 1.7 copy-done
  137.8 3.6 %convolution_convert_fusion.1 = bf16[768,768]{1,0:T(8,128)(2,1)} fusion(bf16[768,2048]{1,0:T(8,128)(2,1)S(1)} %bitcast.19), kind=kOutput, calls=%fused_computation.18 | convolution fusion | flops 2416508928 | bytes 4325376 | tf_op jit(solution)/shard_map/kfd,kgd->kfg/dot_general | solution.py:30
  141.4 7.5 %add_convert_fusion.1 = bf16[768,2048]{1,0:T(8,128)(2,1)S(1)} fusion(bf16[768,2048]{1,0:T(8,128)(2,1)} %bitcast.20, bf16[768,768]{1,0:T(8,128)(2,1)} %convolution_convert_fusion.1), kind=kOutput, calls=%fused_computation.5 | convolution fusion | flops 3331129344 | bytes 7471104 | tf_op jit(solution)/shard_map/kfg,kgd->kfd/dot_general | solution.py:21
  148.9 0.0 copy-start.1
  148.9 1.7 copy-done.1
  150.5 3.6 %convolution_convert_fusion = bf16[768,768]{1,0:T(8,128)(2,1)} fusion(bf16[768,2048]{1,0:T(8,128)(2,1)S(1)} %add_convert_fusion.1), kind=kOutput, calls=%fused_computation.17 | convolution fusion | flops 2416508928 | bytes 4325376 | tf_op jit(solution)/shard_map/kfd,kgd->kfg/dot_general | solution.py:30
  154.2 7.5 %add_convert_fusion = bf16[768,2048]{1,0:T(8,128)(2,1)S(1)} fusion(bf16[768,2048]{1,0:T(8,128)(2,1)} %copy-done.1, bf16[768,768]{1,0:T(8,128)(2,1)} %convolution_convert_fusion), kind=kOutput, calls=%fused_computation.4 | convolution fusion | flops 3331129344 | bytes 7471104 | tf_op jit(solution)/shard_map/kfg,kgd->kfd/dot_general | solution.py:21
  161.7 43.2 %all_to_all.11 = bf16[1,32,24,2048]{3,2,0,1:T(8,128)(2,1)S(1)} all-to-all(bf16[1,32,24,2048]{3,2,0,1:T(8,128)(2,1)S(1)} %bitcast.21), channel_id=1, replica_groups=mesh['expert'=8,'dp'=32] {'dp'}, dimensions={1} | all-to-all | bytes 6291456 | tf_op jit(solution)/shard_map/all_to_all | solution.py:55
  204.8 1.3 multiply_convert_fusion
Async XLA Ops:
  136.1 1.7 copy-start
  148.9 1.7 copy-start.1
where the time goes:
time: 206 us
  blocking collectives  168 us (82%)
  matrix products  22.2 us (11%)
  other arithmetic  10 us (5%)
  local copies, waits for them, and re-layouts  3.69 us (2%)
  between operations  2.11 us (1%)
    psum x1, blocking collectives, shards(): total = lax.psum(jnp.sum(wide_grads * wide_grads), ('expert', 'dp'))  81.4 us
    all_to_all x1, blocking collectives, shards(): lax.all_to_all(sending, 'dp', split_axis=1, concat_axis=1, tiled=True)  43.6 us
    all_to_all x1, blocking collectives, shards(): lax.all_to_all(ortho.reshape(items, count_dp, shard_rows, width), 'dp', s...  43.2 us
    dot_general x2, matrix products, newton_step(): jnp.einsum('kfg,kgd->kfd', mix, full, preferred_element_type=jnp.float32)  14.9 us
    dot_general x2, matrix products, orthogonalize(): jnp.einsum('kfd,kgd->kfg', iterate, iterate, preferred_element_type=jnp.f...  7.28 us

commit v1 on v0

v1 whole, which is shorter than its diff:
```python
import functools
import math

import jax
import jax.numpy as jnp
from jax import lax
from jax.experimental import pallas as pl
from jax.experimental.pallas import tpu as pltpu
from jax.sharding import PartitionSpec as P

lin_coef = 3.4445
cub_coef = -4.775
quint_coef = 2.0315
epsilon = 1e-07
momentum_rate = 0.95

MESH = pl.DeviceIdType.MESH
F32 = jnp.float32
BF16 = jnp.bfloat16

SIDE = 4
CHIPS = SIDE * SIDE
PLANES = 8
DP = 2 * CHIPS
MATS = 12
ROWS = 24
WIDTH = 2048
FULL = ROWS * DP
CHUNKS = 4
COLS = WIDTH // CHUNKS
HALF = COLS // 2
PIECE = 2 * ROWS
SUM_PEERS = 16


def owner_of(k):
    y = k // (SIDE - 1)
    x = lax.rem(y + 1 + lax.rem(k, SIDE - 1), SIDE)
    return (y * SIDE + x) * 2


def stack_halves(wide):
    return jnp.concatenate([wide[:, :HALF], wide[:, HALF:]], axis=0)


def kernel(
    g_hbm, m_hbm, nm_hbm, up_hbm,
    g_v, m_v, nm_v, up_v, lead, recv, full, acc, gram, mix, prod, mix2, norm_sq, outgoing, returned, part_a, part_b,
    g_sem, m_sem, out_sem, sum_send, sum_recv, lead_send, lead_recv, ret_send, ret_recv,
):
    z = lax.axis_index("expert")
    me = lax.axis_index("dp")
    chip = me // 2
    core = lax.rem(me, 2)
    my_y = chip // SIDE
    my_x = lax.rem(chip, SIDE)
    my_j = lax.rem(my_x - my_y - 1 + 2 * SIDE, SIDE)
    is_owner = jnp.logical_and(core == 0, my_j < SIDE - 1)
    my_k = my_y * (SIDE - 1) + my_j

    line = z * 2 + core

    def peer_a(i):
        p = lax.rem(line + i, SUM_PEERS)
        return (p // 2, chip * 2 + lax.rem(p, 2))

    def peer_b(i):
        p = lax.rem(chip + i, SUM_PEERS)
        return (z, p * 2 + core)

    for k in range(4):
        part = pl.ds(3 * k, 3)
        pltpu.make_async_copy(g_hbm.at[part], g_v.at[part], g_sem.at[k]).start()
    load_m = pltpu.make_async_copy(m_hbm, m_v, m_sem)
    load_m.start()

    barrier = pltpu.get_barrier_semaphore()

    def greet(i, carry):
        pl.semaphore_signal(barrier, inc=1, device_id=peer_a(i), device_id_type=MESH)
        pl.semaphore_signal(barrier, inc=1, device_id=peer_b(i), device_id_type=MESH)
        return carry

    lax.fori_loop(1, SUM_PEERS, greet, 0)

    total = jnp.zeros((8, 128), F32)
    for k in range(4):
        part = pl.ds(3 * k, 3)
        pltpu.make_async_copy(g_hbm.at[part], g_v.at[part], g_sem.at[k]).wait()

        def squares(i, carry):
            wide = g_v[i // 4, :, pl.ds(pl.multiple_of(lax.rem(i, 4) * COLS, COLS), COLS)].astype(F32)
            wide = wide * wide
            wide = wide[0:8] + wide[8:16] + wide[16:24]
            wide = wide[:, 0:256] + wide[:, 256:512]
            return carry + (wide[:, 0:128] + wide[:, 128:256])

        total = lax.fori_loop(12 * k, 12 * k + 12, squares, total, unroll=4)

    pl.semaphore_wait(barrier, 2 * (SUM_PEERS - 1))

    def exchange(total, part, slot, peer, stage):
        part[slot] = total

        def send(i, carry):
            pltpu.make_async_remote_copy(
                src_ref=part.at[slot], dst_ref=part.at[slot], send_sem=sum_send.at[stage], recv_sem=sum_recv.at[stage],
                device_id=peer(i), device_id_type=MESH,
            ).start()
            return carry

        lax.fori_loop(1, SUM_PEERS, send, 0)
        others = part.at[pl.ds(0, SUM_PEERS - 1)]
        pltpu.make_async_copy(others, others, sum_recv.at[stage]).wait()
        return jnp.sum(part[...], axis=0)

    total = exchange(total, part_a, line, peer_a, 0)
    total = exchange(total, part_b, chip, peer_b, 1)
    count = MATS * PLANES * FULL * WIDTH
    mean = jnp.sum(total, axis=(0, 1), keepdims=True) / count
    clip = 1.0 / jnp.maximum(jnp.sqrt(mean), 1.0)

    load_m.wait()

    def send_chunk(c, carry):
        columns = pl.ds(pl.multiple_of(c * COLS, COLS), COLS)

        def send_one(i, carry):
            k = lax.rem(i + me, MATS)
            dest = owner_of(k)
            scaled = clip * g_v[k, :, columns].astype(F32)
            moment = momentum_rate * m_v[k, :, columns].astype(F32) + scaled
            piece = stack_halves(scaled + momentum_rate * moment).astype(BF16)
            lead[c, k] = piece

            @pl.when(dest == me)
            def _():
                recv[c, me] = piece

            @pl.when(dest != me)
            def _():
                pltpu.make_async_remote_copy(
                    src_ref=lead.at[c, k], dst_ref=recv.at[c, me], send_sem=lead_send, recv_sem=lead_recv.at[c],
                    device_id=(z, dest), device_id_type=MESH,
                ).start()

            return carry

        return lax.fori_loop(0, MATS, send_one, carry)

    lax.fori_loop(0, CHUNKS, send_chunk, 0)

    def momentum_step(i, carry):
        k = i // CHUNKS
        columns = pl.ds(pl.multiple_of(lax.rem(i, CHUNKS) * COLS, COLS), COLS)
        scaled = clip * g_v[k, :, columns].astype(F32)
        nm_v[k, :, columns] = (momentum_rate * m_v[k, :, columns].astype(F32) + scaled).astype(BF16)
        return carry

    lax.fori_loop(0, MATS * CHUNKS, momentum_step, 0)
    store_nm = pltpu.make_async_copy(nm_v, nm_hbm, out_sem.at[0])
    store_nm.start()

    @pl.when(is_owner)
    def _():
        norm_sq[...] = jnp.zeros_like(norm_sq)

        def collect(c, carry):
            others = recv.at[c, pl.ds(0, DP - 1)]
            pltpu.make_async_copy(others, others, lead_recv.at[c]).wait()
            left = pl.ds(pl.multiple_of(c * COLS, COLS), HALF)
            right = pl.ds(pl.multiple_of(c * COLS + HALF, HALF), HALF)

            def unpack(j, total):
                one = recv[c, 2 * j].astype(F32)
                two = recv[c, 2 * j + 1].astype(F32)
                rows = pl.ds(pl.multiple_of(j * PIECE, PIECE), PIECE)
                full[rows, left] = jnp.concatenate([one[:ROWS], two[:ROWS]], axis=0).astype(BF16)
                full[rows, right] = jnp.concatenate([one[ROWS:], two[ROWS:]], axis=0).astype(BF16)
                both = one * one + two * two
                both = both[:, :128] + both[:, 128:]
                return total + (both[0:8] + both[8:16] + both[16:24] + both[24:32] + both[32:40] + both[40:48])

            total = lax.fori_loop(0, DP // 2, unpack, jnp.zeros((8, 128), F32))
            norm_sq[...] += total
            columns = pl.ds(pl.multiple_of(c * COLS, COLS), COLS)
            for n in range(3):
                rows = pl.ds(256 * n, 256)
                new = lax.dot_general(
                    full[:, columns], full[rows, columns], (((1,), (1,)), ((), ())), preferred_element_type=F32
                )

                @pl.when(c == 0)
                def _():
                    acc[:, rows] = new

                @pl.when(c != 0)
                def _():
                    acc[:, rows] += new

            return carry

        lax.fori_loop(0, CHUNKS, collect, 0)

        norm = jnp.sqrt(jnp.sum(norm_sq[...], axis=(0, 1), keepdims=True)) + epsilon
        inverse = 1.0 / norm
        gram[...] = (acc[...] * inverse * inverse).astype(BF16)

        def product(left, right, n):
            return jnp.dot(left[...], right[:, pl.ds(256 * n, 256)], preferred_element_type=F32)

        def block(ref, n):
            return ref[:, pl.ds(256 * n, 256)].astype(F32)

        for n in range(3):
            cols = pl.ds(256 * n, 256)
            mix[:, cols] = (cub_coef * block(gram, n) + quint_coef * product(gram, gram, n)).astype(BF16)
        for n in range(3):
            cols = pl.ds(256 * n, 256)
            new = product(mix, gram, n)
            prod[:, cols] = new.astype(BF16)
            acc[:, cols] = lin_coef * lin_coef * block(gram, n) + 2.0 * lin_coef * new
        for n in range(3):
            cols = pl.ds(256 * n, 256)
            gram[:, cols] = (acc[:, cols] + product(mix, prod, n)).astype(BF16)
        for n in range(3):
            cols = pl.ds(256 * n, 256)
            mix2[:, cols] = (cub_coef * block(gram, n) + quint_coef * product(gram, gram, n)).astype(BF16)
        for n in range(3):
            cols = pl.ds(256 * n, 256)
            prod[:, cols] = (lin_coef * (block(mix, n) + block(mix2, n)) + product(mix2, mix, n)).astype(BF16)

        scale = inverse * (0.2 * math.sqrt(max(FULL, WIDTH)))

        def give_back(c, carry):
            for half in range(2):
                columns = pl.ds(pl.multiple_of(c * COLS + half * HALF, HALF), HALF)
                right = full[:, columns]
                new = jnp.dot(prod[...], right, preferred_element_type=F32)
                new = (new + lin_coef * lin_coef * right.astype(F32)) * scale
                for d in range(0, DP, 2):
                    rows = slice(half * ROWS, half * ROWS + ROWS)
                    outgoing[c, d, rows] = new[d * ROWS : (d + 1) * ROWS].astype(BF16)
                    outgoing[c, d + 1, rows] = new[(d + 1) * ROWS : (d + 2) * ROWS].astype(BF16)

            returned[c, my_k] = outgoing[c, me]

            def send(i, carry):
                dest = lax.rem(me + i, DP)
                pltpu.make_async_remote_copy(
                    src_ref=outgoing.at[c, dest], dst_ref=returned.at[c, my_k], send_sem=ret_send,
                    recv_sem=ret_recv.at[c], device_id=(z, dest), device_id_type=MESH,
                ).start()
                return carry

            return lax.fori_loop(1, DP, send, carry)

        lax.fori_loop(0, CHUNKS, give_back, 0)

    def finish(c, carry):
        @pl.when(is_owner)
        def _():
            others = returned.at[c, pl.ds(0, MATS - 1)]
            pltpu.make_async_copy(others, others, ret_recv.at[c]).wait()

        @pl.when(jnp.logical_not(is_owner))
        def _():
            every = returned.at[c]
            pltpu.make_async_copy(every, every, ret_recv.at[c]).wait()

        left = pl.ds(pl.multiple_of(c * COLS, COLS), HALF)
        right = pl.ds(pl.multiple_of(c * COLS + HALF, HALF), HALF)

        def unpack(k, carry):
            piece = returned[c, k].astype(F32)
            up_v[k, :, left] = piece[:ROWS].astype(BF16)
            up_v[k, :, right] = piece[ROWS:].astype(BF16)
            return carry

        return lax.fori_loop(0, MATS, unpack, carry)

    lax.fori_loop(0, CHUNKS, finish, 0)
    store_up = pltpu.make_async_copy(up_v, up_hbm, out_sem.at[1])
    store_up.start()

    for stage, part in ((0, part_a), (1, part_b)):
        others = part.at[pl.ds(0, SUM_PEERS - 1)]
        pltpu.make_async_copy(others, others, sum_send.at[stage]).wait()

    @pl.when(is_owner)
    def _():
        others = lead.at[:, pl.ds(0, MATS - 1)]
        pltpu.make_async_copy(others, others, lead_send).wait()
        others = outgoing.at[:, pl.ds(0, DP - 1)]
        pltpu.make_async_copy(others, others, ret_send).wait()

    @pl.when(jnp.logical_not(is_owner))
    def _():
        pltpu.make_async_copy(lead, lead, lead_send).wait()

    store_nm.wait()
    store_up.wait()


def shards(grads, momentum):
    shape = grads.shape
    flat = (MATS, ROWS, WIDTH)
    out = jax.ShapeDtypeStruct(flat, BF16)
    square = (FULL, FULL)
    new_momentum, update = pl.pallas_call(
        kernel,
        out_shape=(out, out),
        in_specs=[pl.BlockSpec(memory_space=pl.ANY)] * 2,
        out_specs=(pl.BlockSpec(memory_space=pl.ANY),) * 2,
        scratch_shapes=[
            pltpu.VMEM(flat, BF16),
            pltpu.VMEM(flat, BF16),
            pltpu.VMEM(flat, BF16),
            pltpu.VMEM(flat, BF16),
            pltpu.VMEM((CHUNKS, MATS, PIECE, HALF), BF16),
            pltpu.VMEM((CHUNKS, DP, PIECE, HALF), BF16),
            pltpu.VMEM((FULL, WIDTH), BF16),
            pltpu.VMEM(square, F32),
            pltpu.VMEM(square, BF16),
            pltpu.VMEM(square, BF16),
            pltpu.VMEM(square, BF16),
            pltpu.VMEM(square, BF16),
            pltpu.VMEM((8, 128), F32),
            pltpu.VMEM((CHUNKS, DP, PIECE, HALF), BF16),
            pltpu.VMEM((CHUNKS, MATS, PIECE, HALF), BF16),
            pltpu.VMEM((SUM_PEERS, 8, 128), F32),
            pltpu.VMEM((SUM_PEERS, 8, 128), F32),
            pltpu.SemaphoreType.DMA((4,)),
            pltpu.SemaphoreType.DMA,
            pltpu.SemaphoreType.DMA((2,)),
            pltpu.SemaphoreType.DMA((2,)),
            pltpu.SemaphoreType.DMA((2,)),
            pltpu.SemaphoreType.DMA,
            pltpu.SemaphoreType.DMA((CHUNKS,)),
            pltpu.SemaphoreType.DMA,
            pltpu.SemaphoreType.DMA((CHUNKS,)),
        ],
        compiler_params=pltpu.CompilerParams(
            collective_id=0, has_side_effects=True, vmem_limit_bytes=48 * 1024 * 1024
        ),
        name="muon_step",
    )(grads.reshape(flat), momentum.reshape(flat))
    return new_momentum.reshape(shape), update.reshape(shape)


def solution(mesh):
    placed = (P("expert", None, "dp", None), P("expert", None, "dp", None))
    return jax.shard_map(
        shards,
        mesh=mesh,
        in_specs=placed,
        out_specs=(P("expert", None, "dp", None), P("expert", None, "dp", None)),
        check_vma=False,
    )
```

time: 206 us -> 78.5 us (0.38)
  blocking collectives: 168 us -> 0 us
  Pallas kernels: 0 us -> 73.1 us
  matrix products: 22.2 us -> 0 us
  other arithmetic: 10 us -> 0 us
    all_to_all x2 -> x0, blocking collectives: 86.7 us -> none  [the longest x1 43.6 us: shards(): lax.all_to_all(sending, 'dp', split_axis=1, concat_axis=1, tiled=True)]
    psum x1 -> x0, blocking collectives: 81.4 us -> none  [shards(): total = lax.psum(jnp.sum(wide_grads * wide_grads), ('expert', 'dp'))]
    pallas_call x0 -> x1, Pallas kernels: none -> 73.1 us  [shards(): pl.pallas_call(kernel, out_shape=(out, out), in_specs=[pl.BlockSpec(memor...]
    dot_general x4 -> x0, matrix products: 22.2 us -> none  [the longest x2 14.9 us: newton_step(): jnp.einsum('kfg,kgd->kfd', mix, full, preferred_element_type=jnp.float32)]
    convert_element_type x3 -> x0, other arithmetic: 5.31 us -> none  [the longest x1 3.29 us: shards(): lead = (clip * wide_grads + momentum_rate * moment).astype(jnp.bfloat16)]
    reduce_sum x2 -> x0, other arithmetic: 4.7 us -> none  [the longest x1 2.48 us: shards(): total = lax.psum(jnp.sum(wide_grads * wide_grads), ('expert', 'dp'))]
    unnamed x4 -> x6, local copies, waits for them, and re-layouts: 3.32 us -> 4.56 us
where the time goes in v1:
time: 78.5 us; the launch traced here: 78.3 us
  Pallas kernels  73.1 us (93%)
  local copies, waits for them, and re-layouts  4.56 us (6%)
    pallas_call x1, Pallas kernels, shards(): pl.pallas_call(kernel, out_shape=(out, out), in_specs=[pl.BlockSpec(memor...  73.1 us
    unnamed x6, local copies, waits for them, and re-layouts  4.56 us

profile of v1, /device:TPU:1, one launch (start us, length us, event | category | flops | bytes accessed | tf_op | source)
XLA Modules:
  0.0 78.3 jit_solution(5359704775105232288)
XLA Ops:
  0.6 0.0 copy-start
  0.6 1.3 %copy-done = bf16[4,3,24,2048]{3,2,1,0:T(8,128)(2,1)S(1)} copy-done((bf16[4,3,24,2048]{3,2,1,0:T(8,128)(2,1)S(1)}, bf16[4,3,24,2048]{3,2,1,0:T(8,128)(2,1)}, u32[]{:S(2)}) %copy-start) | copy-done | bytes 1179672
  1.9 0.0 copy-start.1
  1.9 1.3 %copy-done.1 = bf16[4,3,24,2048]{3,2,1,0:T(8,128)(2,1)S(1)} copy-done((bf16[4,3,24,2048]{3,2,1,0:T(8,128)(2,1)S(1)}, bf16[4,3,24,2048]{3,2,1,0:T(8,128)(2,1)}, u32[]{:S(2)}) %copy-start.1) | copy-done | bytes 1179672
  3.2 73.1 %muon_step.1 = (bf16[12,24,2048]{2,1,0:T(8,128)(2,1)S(1)}, bf16[12,24,2048]{2,1,0:T(8,128)(2,1)S(1)}) custom-call(bf16[12,24,2048]{2,1,0:T(8,128)(2,1)S(1)} %bitcast.4, bf16[12,24,2048]{2,1,0:T(8,128)(2,1)S(1)} %bitcast.5), custom_call_target="tpu_custom_call" | custom-call | tf_op jit(solution)/shard_map/muon_step/pallas_call | solution.py:310
  76.3 1.0 %copy.6 = bf16[4,3,24,2048]{3,2,1,0:T(8,128)(2,1)} copy(bf16[4,3,24,2048]{3,2,1,0:T(8,128)(2,1)S(1)} %bitcast.7) | data formatting | bytes 2359296
  77.3 1.0 %copy.7 = bf16[4,3,24,2048]{3,2,1,0:T(8,128)(2,1)} copy(bf16[4,3,24,2048]{3,2,1,0:T(8,128)(2,1)S(1)} %bitcast.6) | data formatting | bytes 2359296
Async XLA Ops:
  0.6 1.3 %copy-start = (bf16[4,3,24,2048]{3,2,1,0:T(8,128)(2,1)S(1)}, bf16[4,3,24,2048]{3,2,1,0:T(8,128)(2,1)}, u32[]{:S(2)}) copy-start(bf16[4,3,24,2048]{3,2,1,0:T(8,128)(2,1)} %param.2) | copy-start | bytes 3538948
  1.9 1.3 %copy-start.1 = (bf16[4,3,24,2048]{3,2,1,0:T(8,128)(2,1)S(1)}, bf16[4,3,24,2048]{3,2,1,0:T(8,128)(2,1)}, u32[]{:S(2)}) copy-start(bf16[4,3,24,2048]{3,2,1,0:T(8,128)(2,1)} %param.3) | copy-start | bytes 3538948

commit v2 on v1

v2 whole, which is shorter than its diff:
```python
import functools
import math

import jax
import jax.numpy as jnp
from jax import lax
from jax.experimental import pallas as pl
from jax.experimental.pallas import tpu as pltpu
from jax.sharding import PartitionSpec as P

lin_coef = 3.4445
cub_coef = -4.775
quint_coef = 2.0315
epsilon = 1e-07
momentum_rate = 0.95

MESH = pl.DeviceIdType.MESH
F32 = jnp.float32
BF16 = jnp.bfloat16

SIDE = 4
CHIPS = SIDE * SIDE
PLANES = 8
DP = 2 * CHIPS
MATS = 12
ROWS = 24
WIDTH = 2048
FULL = ROWS * DP
COLS = 512
NARROW = 256
PIECE = 2 * ROWS
SUM_PEERS = 16
GATHER = ((0, NARROW), (NARROW, NARROW), (512, COLS), (1024, COLS), (1536, COLS))
SPREAD = ((0, NARROW), (512, COLS), (1024, COLS), (1536, COLS), (NARROW, NARROW))


def owner_of(k):
    y = k // (SIDE - 1)
    x = lax.rem(y + 1 + lax.rem(k, SIDE - 1), SIDE)
    return (y * SIDE + x) * 2


def stack_halves(wide):
    half = wide.shape[1] // 2
    return jnp.concatenate([wide[:, :half], wide[:, half:]], axis=0)


def pieces(count, columns):
    return pltpu.VMEM((count, PIECE, columns // 2), BF16)


def kernel(
    g_hbm, m_hbm, nm_hbm, up_hbm,
    g_v, m_v, nm_v, up_v, raw, recv_g, recv_m, leads, recvs, full, acc, gram, mix, prod, mix2, outgoing, returned, part_a, part_b,
    g_sem, m_sem, out_sem, sum_send, sum_recv, raw_send, raw_recv, lead_send, lead_recv, ret_send, ret_recv,
):
    z = lax.axis_index("expert")
    me = lax.axis_index("dp")
    chip = me // 2
    core = lax.rem(me, 2)
    my_y = chip // SIDE
    my_x = lax.rem(chip, SIDE)
    my_j = lax.rem(my_x - my_y - 1 + 2 * SIDE, SIDE)
    is_owner = jnp.logical_and(core == 0, my_j < SIDE - 1)
    my_k = my_y * (SIDE - 1) + my_j

    line = z * 2 + core

    def peer_a(i):
        p = lax.rem(line + i, SUM_PEERS)
        return (p // 2, chip * 2 + lax.rem(p, 2))

    def peer_b(i):
        p = lax.rem(chip + i, SUM_PEERS)
        return (z, p * 2 + core)

    for k in range(4):
        part = pl.ds(3 * k, 3)
        pltpu.make_async_copy(g_hbm.at[part], g_v.at[part], g_sem.at[k]).start()
    load_m = pltpu.make_async_copy(m_hbm, m_v, m_sem)
    load_m.start()

    barrier = pltpu.get_barrier_semaphore()
    for i in range(1, SUM_PEERS):
        pl.semaphore_signal(barrier, inc=1, device_id=peer_a(i), device_id_type=MESH)
        pl.semaphore_signal(barrier, inc=1, device_id=peer_b(i), device_id_type=MESH)

    @pl.when(is_owner)
    def _():
        for i in range(1, CHIPS):
            other = (z, lax.rem(chip + i, CHIPS) * 2 + 1)
            pl.semaphore_signal(barrier, inc=1, device_id=other, device_id_type=MESH)

    total = jnp.zeros((8, 128), F32)
    for k in range(4):
        part = pl.ds(3 * k, 3)
        pltpu.make_async_copy(g_hbm.at[part], g_v.at[part], g_sem.at[k]).wait()

        def squares(i, carry):
            wide = g_v[i // 4, :, pl.ds(pl.multiple_of(lax.rem(i, 4) * COLS, COLS), COLS)].astype(F32)
            wide = wide * wide
            wide = wide[0:8] + wide[8:16] + wide[16:24]
            wide = wide[:, 0:256] + wide[:, 256:512]
            return carry + (wide[:, 0:128] + wide[:, 128:256])

        total = lax.fori_loop(12 * k, 12 * k + 12, squares, total, unroll=4)

    others_owning = jnp.where(my_j < SIDE - 1, MATS - 1, MATS)
    pl.semaphore_wait(barrier, 2 * (SUM_PEERS - 1) + jnp.where(core == 1, others_owning, 0))

    def send_sum(total, part, slot, peer, stage):
        part[slot] = total
        for i in range(1, SUM_PEERS):
            pltpu.make_async_remote_copy(
                src_ref=part.at[slot], dst_ref=part.at[slot], send_sem=sum_send.at[stage], recv_sem=sum_recv.at[stage],
                device_id=peer(i), device_id_type=MESH,
            ).start()

    def take_sum(part, stage):
        others = part.at[pl.ds(0, SUM_PEERS - 1)]
        pltpu.make_async_copy(others, others, sum_recv.at[stage]).wait()
        return jnp.sum(part[...], axis=0)

    def push(piece, buffer, slot, landing, k, send_sem, recv_sem):
        dest = owner_of(k)
        buffer[slot] = piece

        @pl.when(dest == me)
        def _():
            landing[me] = piece

        @pl.when(dest != me)
        def _():
            pltpu.make_async_remote_copy(
                src_ref=buffer.at[slot], dst_ref=landing.at[me], send_sem=send_sem, recv_sem=recv_sem,
                device_id=(z, dest), device_id_type=MESH,
            ).start()

    send_sum(total, part_a, line, peer_a, 0)
    load_m.wait()

    def send_raw(i, carry):
        k = lax.rem(i + me, MATS)
        push(stack_halves(g_v[k, :, :NARROW].astype(F32)).astype(BF16), raw, k, recv_g, k, raw_send, raw_recv.at[0])
        push(stack_halves(m_v[k, :, :NARROW].astype(F32)).astype(BF16), raw, MATS + k, recv_m, k, raw_send, raw_recv.at[1])
        return carry

    lax.fori_loop(0, MATS // 2, send_raw, 0)
    total = take_sum(part_a, 0)
    send_sum(total, part_b, chip, peer_b, 1)
    lax.fori_loop(MATS // 2, MATS, send_raw, 0)
    total = take_sum(part_b, 1)
    count = MATS * PLANES * FULL * WIDTH
    mean = jnp.sum(total, axis=(0, 1), keepdims=True) / count
    clip = 1.0 / jnp.maximum(jnp.sqrt(mean), 1.0)

    def combine(g, m):
        scaled = clip * g.astype(F32)
        moment = momentum_rate * m.astype(F32) + scaled
        return moment, scaled + momentum_rate * moment

    for c in range(1, len(GATHER)):
        columns = pl.ds(*GATHER[c])

        def send_lead(i, carry, columns=columns, c=c):
            k = lax.rem(i + me, MATS)
            piece = stack_halves(combine(g_v[k, :, columns], m_v[k, :, columns])[1]).astype(BF16)
            push(piece, leads[c - 1], k, recvs[c - 1], k, lead_send.at[c - 1], lead_recv.at[c - 1])
            return carry

        lax.fori_loop(0, MATS, send_lead, 0)

    def momentum_step(i, carry):
        k = i // 4
        columns = pl.ds(pl.multiple_of(lax.rem(i, 4) * COLS, COLS), COLS)
        nm_v[k, :, columns] = combine(g_v[k, :, columns], m_v[k, :, columns])[0].astype(BF16)
        return carry

    lax.fori_loop(0, 4 * MATS, momentum_step, 0, unroll=4)
    store_nm = pltpu.make_async_copy(nm_v, nm_hbm, out_sem.at[0])
    store_nm.start()

    @pl.when(is_owner)
    def _():
        def unpack(one, two, j, start, total):
            half = one.shape[1]
            rows = pl.ds(pl.multiple_of(j * PIECE, PIECE), PIECE)
            full[rows, pl.ds(start, half)] = jnp.concatenate([one[:ROWS], two[:ROWS]], axis=0).astype(BF16)
            full[rows, pl.ds(start + half, half)] = jnp.concatenate([one[ROWS:], two[ROWS:]], axis=0).astype(BF16)
            both = one * one + two * two
            if half == 256:
                both = both[:, :128] + both[:, 128:]
            return total + (both[0:8] + both[8:16] + both[16:24] + both[24:32] + both[32:40] + both[40:48])

        def lower(n):
            return pl.ds(256 * n, FULL - 256 * n), pl.ds(256 * n, 256)

        def grams(columns):
            for n in range(3):
                low, cols = lower(n)
                new = lax.dot_general(
                    full[low, columns], full[cols, columns], (((1,), (1,)), ((), ())), preferred_element_type=F32
                )
                yield low, cols, new

        for stage, landing in ((0, recv_g), (1, recv_m)):
            others = landing.at[pl.ds(0, DP - 1)]
            pltpu.make_async_copy(others, others, raw_recv.at[stage]).wait()

        def unpack_raw(j, total):
            one = combine(recv_g[2 * j], recv_m[2 * j])[1].astype(BF16).astype(F32)
            two = combine(recv_g[2 * j + 1], recv_m[2 * j + 1])[1].astype(BF16).astype(F32)
            return unpack(one, two, j, 0, total)

        squared = lax.fori_loop(0, DP // 2, unpack_raw, jnp.zeros((8, 128), F32), unroll=4)
        for low, cols, new in grams(pl.ds(*GATHER[0])):
            acc[low, cols] = new

        for c in range(1, len(GATHER)):
            landing = recvs[c - 1]
            others = landing.at[pl.ds(0, DP - 1)]
            pltpu.make_async_copy(others, others, lead_recv.at[c - 1]).wait()

            def unpack_lead(j, total, landing=landing, start=GATHER[c][0]):
                return unpack(landing[2 * j].astype(F32), landing[2 * j + 1].astype(F32), j, start, total)

            squared = lax.fori_loop(0, DP // 2, unpack_lead, squared, unroll=4)
            for low, cols, new in grams(pl.ds(*GATHER[c])):
                acc[low, cols] += new

        norm = jnp.sqrt(jnp.sum(squared, axis=(0, 1), keepdims=True)) + epsilon
        inverse = 1.0 / norm

        def put(ref, n, value):
            value = value.astype(BF16)
            low, cols = lower(n)
            ref[low, cols] = value
            for m in range(n + 1, 3):
                ref[cols, pl.ds(256 * m, 256)] = value[256 * (m - n) : 256 * (m - n) + 256].T

        def product(left, right, n):
            low, cols = lower(n)
            return jnp.dot(left[low, :], right[:, cols], preferred_element_type=F32)

        def block(ref, n):
            return ref[lower(n)].astype(F32)

        for n in range(3):
            put(gram, n, acc[lower(n)] * inverse * inverse)
        for n in range(3):
            put(mix, n, cub_coef * block(gram, n) + quint_coef * product(gram, gram, n))
        for n in range(3):
            new = product(mix, gram, n)
            put(prod, n, new)
            acc[lower(n)] = lin_coef * lin_coef * block(gram, n) + 2.0 * lin_coef * new
        for n in range(3):
            put(gram, n, acc[lower(n)] + product(mix, prod, n))
        for n in range(3):
            put(mix2, n, cub_coef * block(gram, n) + quint_coef * product(gram, gram, n))
        for n in range(3):
            put(prod, n, lin_coef * (block(mix, n) + block(mix2, n)) + product(mix2, mix, n))

        scale = inverse * (0.2 * math.sqrt(max(FULL, WIDTH)))

        for c, (start, width) in enumerate(SPREAD):
            half = width // 2
            parts = []
            for columns in (pl.ds(start, half), pl.ds(start + half, half)):
                right = full[:, columns]
                new = jnp.dot(prod[...], right, preferred_element_type=F32)
                parts.append((new + lin_coef * lin_coef * right.astype(F32)) * scale)
            for d in range(DP):
                rows = slice(d * ROWS, (d + 1) * ROWS)
                outgoing[c][d] = jnp.concatenate([part[rows] for part in parts], axis=0).astype(BF16)

            returned[c][my_k] = outgoing[c][me]

            def send(i, carry, c=c):
                dest = lax.rem(me + i, DP)
                pltpu.make_async_remote_copy(
                    src_ref=outgoing[c].at[dest], dst_ref=returned[c].at[my_k], send_sem=ret_send.at[c],
                    recv_sem=ret_recv.at[c], device_id=(z, dest), device_id_type=MESH,
                ).start()
                return carry

            lax.fori_loop(1, DP, send, 0)

    stores = []
    for c, (start, width) in enumerate(SPREAD):
        landing = returned[c]

        @pl.when(is_owner)
        def _():
            others = landing.at[pl.ds(0, MATS - 1)]
            pltpu.make_async_copy(others, others, ret_recv.at[c]).wait()

        @pl.when(jnp.logical_not(is_owner))
        def _():
            pltpu.make_async_copy(landing, landing, ret_recv.at[c]).wait()

        def unpack_result(k, carry, landing=landing, start=start, half=width // 2):
            piece = landing[k].astype(F32)
            up_v[k, :, pl.ds(start, half)] = piece[:ROWS].astype(BF16)
            up_v[k, :, pl.ds(start + half, half)] = piece[ROWS:].astype(BF16)
            return carry

        lax.fori_loop(0, MATS, unpack_result, 0, unroll=4)
        columns = pl.ds(start, width)
        stores.append(pltpu.make_async_copy(up_v.at[:, :, columns], up_hbm.at[:, :, columns], out_sem.at[1 + c]))
        stores[-1].start()

    for stage, part in ((0, part_a), (1, part_b)):
        others = part.at[pl.ds(0, SUM_PEERS - 1)]
        pltpu.make_async_copy(others, others, sum_send.at[stage]).wait()

    @pl.when(is_owner)
    def _():
        others = raw.at[pl.ds(0, 2 * (MATS - 1))]
        pltpu.make_async_copy(others, others, raw_send).wait()
        for c, buffer in enumerate(leads):
            others = buffer.at[pl.ds(0, MATS - 1)]
            pltpu.make_async_copy(others, others, lead_send.at[c]).wait()
        for c, buffer in enumerate(outgoing):
            others = buffer.at[pl.ds(0, DP - 1)]
            pltpu.make_async_copy(others, others, ret_send.at[c]).wait()

    @pl.when(jnp.logical_not(is_owner))
    def _():
        pltpu.make_async_copy(raw, raw, raw_send).wait()
        for c, buffer in enumerate(leads):
            pltpu.make_async_copy(buffer, buffer, lead_send.at[c]).wait()

    store_nm.wait()
    for store in stores:
        store.wait()


def shards(grads, momentum):
    shape = grads.shape
    flat = (MATS, ROWS, WIDTH)
    out = jax.ShapeDtypeStruct(flat, BF16)
    square = (FULL, FULL)
    new_momentum, update = pl.pallas_call(
        kernel,
        out_shape=(out, out),
        in_specs=[pl.BlockSpec(memory_space=pl.ANY)] * 2,
        out_specs=(pl.BlockSpec(memory_space=pl.ANY),) * 2,
        scratch_shapes=[
            pltpu.VMEM(flat, BF16),
            pltpu.VMEM(flat, BF16),
            pltpu.VMEM(flat, BF16),
            pltpu.VMEM(flat, BF16),
            pieces(2 * MATS, NARROW),
            pieces(DP, NARROW),
            pieces(DP, NARROW),
            [pieces(MATS, width) for _, width in GATHER[1:]],
            [pieces(DP, width) for _, width in GATHER[1:]],
            pltpu.VMEM((FULL, WIDTH), BF16),
            pltpu.VMEM(square, F32),
            pltpu.VMEM(square, BF16),
            pltpu.VMEM(square, BF16),
            pltpu.VMEM(square, BF16),
            pltpu.VMEM(square, BF16),
            [pieces(DP, width) for _, width in SPREAD],
            [pieces(MATS, width) for _, width in SPREAD],
            pltpu.VMEM((SUM_PEERS, 8, 128), F32),
            pltpu.VMEM((SUM_PEERS, 8, 128), F32),
            pltpu.SemaphoreType.DMA((4,)),
            pltpu.SemaphoreType.DMA,
            pltpu.SemaphoreType.DMA((1 + len(SPREAD),)),
            pltpu.SemaphoreType.DMA((2,)),
            pltpu.SemaphoreType.DMA((2,)),
            pltpu.SemaphoreType.DMA,
            pltpu.SemaphoreType.DMA((2,)),
            pltpu.SemaphoreType.DMA((len(GATHER) - 1,)),
            pltpu.SemaphoreType.DMA((len(GATHER) - 1,)),
            pltpu.SemaphoreType.DMA((len(SPREAD),)),
            pltpu.SemaphoreType.DMA((len(SPREAD),)),
        ],
        compiler_params=pltpu.CompilerParams(
            collective_id=0, has_side_effects=True, vmem_limit_bytes=51 * 1024 * 1024 + 256 * 1024
        ),
        name="muon_step",
    )(grads.reshape(flat), momentum.reshape(flat))
    return new_momentum.reshape(shape), update.reshape(shape)


def solution(mesh):
    placed = (P("expert", None, "dp", None), P("expert", None, "dp", None))
    return jax.shard_map(
        shards,
        mesh=mesh,
        in_specs=placed,
        out_specs=(P("expert", None, "dp", None), P("expert", None, "dp", None)),
        check_vma=False,
    )
```

time: 78.5 us -> 66.4 us (0.85)
  Pallas kernels: 73.1 us -> 63.7 us
  local copies, waits for them, and re-layouts: 4.56 us -> 2.03 us
    pallas_call x1, Pallas kernels: 73.1 us -> 63.7 us  [shards(): pl.pallas_call(kernel, out_shape=(out, out), in_specs=[pl.BlockSpec(memor...]
    unnamed x6 -> x2, local copies, waits for them, and re-layouts: 4.56 us -> 2.03 us
where the time goes in v2:
time: 66.4 us; the launch traced here: 66.3 us
  Pallas kernels  63.7 us (96%)
  local copies, waits for them, and re-layouts  2.03 us (3%)
    pallas_call x1, Pallas kernels, shards(): pl.pallas_call(kernel, out_shape=(out, out), in_specs=[pl.BlockSpec(memor...  63.7 us
    unnamed x2, local copies, waits for them, and re-layouts  2.03 us

profile of v2, /device:TPU:1, one launch (start us, length us, event | category | flops | bytes accessed | tf_op | source)
XLA Modules:
  0.0 66.3 jit_solution(3759921324759251681)
XLA Ops:
  0.6 63.7 %muon_step.1 = (bf16[12,24,2048]{2,1,0:T(8,128)(2,1)S(1)}, bf16[12,24,2048]{2,1,0:T(8,128)(2,1)S(1)}) custom-call(bf16[12,24,2048]{2,1,0:T(8,128)(2,1)} %bitcast.6, bf16[12,24,2048]{2,1,0:T(8,128)(2,1)} %bitcast.7), custom_call_target="tpu_custom_call" | custom-call | tf_op jit(solution)/shard_map/muon_step/pallas_call | solution.py:343
  64.3 1.0 %copy.6 = bf16[4,3,24,2048]{3,2,1,0:T(8,128)(2,1)} copy(bf16[4,3,24,2048]{3,2,1,0:T(8,128)(2,1)S(1)} %bitcast.5) | data formatting | bytes 2359296
  65.3 1.0 %copy.7 = bf16[4,3,24,2048]{3,2,1,0:T(8,128)(2,1)} copy(bf16[4,3,24,2048]{3,2,1,0:T(8,128)(2,1)S(1)} %bitcast.4) | data formatting | bytes 2359296

commit v3 on v2

--- a/solution.py
+++ b/solution.py
@@ -34,10 +34,28 @@
 SPREAD = ((0, NARROW), (512, COLS), (1024, COLS), (1536, COLS), (NARROW, NARROW))
 
 
-def owner_of(k):
-    y = k // (SIDE - 1)
-    x = lax.rem(y + 1 + lax.rem(k, SIDE - 1), SIDE)
+def hops(step, size):
+    return min(step, size - step)
+
+
+FAR_A = sorted(
+    ((dz, other) for dz in range(PLANES) for other in range(2) if dz or other), key=lambda p: -hops(p[0], PLANES)
+)
+FAR_B = sorted(
+    ((dy, dx) for dy in range(SIDE) for dx in range(SIDE) if dy or dx),
+    key=lambda p: -hops(p[0], SIDE) - hops(p[1], SIDE),
+)
+
+
+def owner_of(k, z):
+    x = k // (SIDE - 1)
+    y = lax.rem(x + z + 1 + lax.rem(k, SIDE - 1), SIDE)
     return (y * SIDE + x) * 2
+
+
+def shifted(z, t, core, sign):
+    step = jnp.where(t == 1, 1, jnp.where(t == 2, 2 - 4 * core, -1))
+    return lax.rem(z + PLANES + sign * step, PLANES)
 
 
 def stack_halves(wide):
@@ -51,8 +69,8 @@
 
 def kernel(
     g_hbm, m_hbm, nm_hbm, up_hbm,
-    g_v, m_v, nm_v, up_v, raw, recv_g, recv_m, leads, recvs, full, acc, gram, mix, prod, mix2, outgoing, returned, part_a, part_b,
-    g_sem, m_sem, out_sem, sum_send, sum_recv, raw_send, raw_recv, lead_send, lead_recv, ret_send, ret_recv,
+    g_v, m_v, nm_v, up_v, raw, recv_g, recv_m, leads, recvs, full, acc, gram, mix, prod, mix2, outgoing, returned, passing, bouncing, part_a, part_b,
+    g_sem, m_sem, out_sem, sum_send, sum_recv, raw_send, raw_recv, lead_send, lead_recv, ret_send, ret_recv, pass_send, pass_recv, bounce_send, bounce_recv,
 ):
     z = lax.axis_index("expert")
     me = lax.axis_index("dp")
@@ -60,19 +78,19 @@
     core = lax.rem(me, 2)
     my_y = chip // SIDE
     my_x = lax.rem(chip, SIDE)
-    my_j = lax.rem(my_x - my_y - 1 + 2 * SIDE, SIDE)
-    is_owner = jnp.logical_and(core == 0, my_j < SIDE - 1)
-    my_k = my_y * (SIDE - 1) + my_j
+    my_t = lax.rem(my_y - my_x - z + 3 * SIDE, SIDE)
+    is_owner = jnp.logical_and(core == 0, my_t != 0)
+    my_k = my_x * (SIDE - 1) + my_t - 1
 
     line = z * 2 + core
 
     def peer_a(i):
-        p = lax.rem(line + i, SUM_PEERS)
-        return (p // 2, chip * 2 + lax.rem(p, 2))
+        dz, other = FAR_A[i - 1]
+        return (lax.rem(z + dz, PLANES), chip * 2 + (1 - core if other else core))
 
     def peer_b(i):
-        p = lax.rem(chip + i, SUM_PEERS)
-        return (z, p * 2 + core)
+        dy, dx = FAR_B[i - 1]
+        return (z, (lax.rem(my_y + dy, SIDE) * SIDE + lax.rem(my_x + dx, SIDE)) * 2 + core)
 
     for k in range(4):
         part = pl.ds(3 * k, 3)
@@ -105,7 +123,7 @@
 
         total = lax.fori_loop(12 * k, 12 * k + 12, squares, total, unroll=4)
 
-    others_owning = jnp.where(my_j < SIDE - 1, MATS - 1, MATS)
+    others_owning = jnp.where(my_t != 0, MATS - 1, MATS)
     pl.semaphore_wait(barrier, 2 * (SUM_PEERS - 1) + jnp.where(core == 1, others_owning, 0))
 
     def send_sum(total, part, slot, peer, stage):
@@ -122,7 +140,7 @@
         return jnp.sum(part[...], axis=0)
 
     def push(piece, buffer, slot, landing, k, send_sem, recv_sem):
-        dest = owner_of(k)
+        dest = owner_of(k, z)
         buffer[slot] = piece
 
         @pl.when(dest == me)
@@ -145,10 +163,9 @@
         push(stack_halves(m_v[k, :, :NARROW].astype(F32)).astype(BF16), raw, MATS + k, recv_m, k, raw_send, raw_recv.at[1])
         return carry
 
-    lax.fori_loop(0, MATS // 2, send_raw, 0)
+    lax.fori_loop(0, MATS, send_raw, 0)
     total = take_sum(part_a, 0)
     send_sum(total, part_b, chip, peer_b, 1)
-    lax.fori_loop(MATS // 2, MATS, send_raw, 0)
     total = take_sum(part_b, 1)
     count = MATS * PLANES * FULL * WIDTH
     mean = jnp.sum(total, axis=(0, 1), keepdims=True) / count
@@ -159,7 +176,20 @@
         moment = momentum_rate * m.astype(F32) + scaled
         return moment, scaled + momentum_rate * moment
 
-    for c in range(1, len(GATHER)):
+    def send_around(i, carry):
+        k = lax.rem(i + me, MATS)
+        t = lax.rem(k, SIDE - 1) + 1
+        columns = pl.ds(*GATHER[1])
+        leads[0][k] = stack_halves(combine(g_v[k, :, columns], m_v[k, :, columns])[1]).astype(BF16)
+        pltpu.make_async_remote_copy(
+            src_ref=leads[0].at[k], dst_ref=passing.at[t - 1, chip], send_sem=lead_send.at[0],
+            recv_sem=pass_recv.at[t - 1], device_id=(shifted(z, t, core, 1), owner_of(k, z) + core), device_id_type=MESH,
+        ).start()
+        return carry
+
+    lax.fori_loop(0, MATS, send_around, 0)
+
+    for c in range(2, len(GATHER)):
         columns = pl.ds(*GATHER[c])
 
         def send_lead(i, carry, columns=columns, c=c):
@@ -169,6 +199,22 @@
             return carry
 
         lax.fori_loop(0, MATS, send_lead, 0)
+
+    @pl.when(my_t == 0)
+    def _():
+        for t in (2, 1, 3):
+            every = passing.at[t - 1]
+            pltpu.make_async_copy(every, every, pass_recv.at[t - 1]).wait()
+
+            def hand_on(i, carry, t=t):
+                source = lax.rem(i + chip, CHIPS)
+                pltpu.make_async_remote_copy(
+                    src_ref=passing.at[t - 1, source], dst_ref=recvs[0].at[source * 2 + core], send_sem=pass_send,
+                    recv_sem=lead_recv.at[0], device_id=(shifted(z, t, core, -1), chip * 2), device_id_type=MESH,
+                ).start()
+                return carry
+
+            lax.fori_loop(0, CHIPS, hand_on, 0)
 
     def momentum_step(i, carry):
         k = i // 4
@@ -216,10 +262,10 @@
         for low, cols, new in grams(pl.ds(*GATHER[0])):
             acc[low, cols] = new
 
-        for c in range(1, len(GATHER)):
+        for c in (*range(2, len(GATHER)), 1):
             landing = recvs[c - 1]
-            others = landing.at[pl.ds(0, DP - 1)]
-            pltpu.make_async_copy(others, others, lead_recv.at[c - 1]).wait()
+            arriving = landing.at[pl.ds(0, DP if c == 1 else DP - 1)]
+            pltpu.make_async_copy(arriving, arriving, lead_recv.at[c - 1]).wait()
 
             def unpack_lead(j, total, landing=landing, start=GATHER[c][0]):
                 return unpack(landing[2 * j].astype(F32), landing[2 * j + 1].astype(F32), j, start, total)
@@ -273,30 +319,52 @@
                 rows = slice(d * ROWS, (d + 1) * ROWS)
                 outgoing[c][d] = jnp.concatenate([part[rows] for part in parts], axis=0).astype(BF16)
 
-            returned[c][my_k] = outgoing[c][me]
+            if c > 0:
+                returned[c][my_k] = outgoing[c][me]
 
             def send(i, carry, c=c):
                 dest = lax.rem(me + i, DP)
+                if c == 0:
+                    landing, sem = bouncing.at[(my_t - 1) * SIDE + my_x], bounce_recv
+                else:
+                    landing, sem = returned[c].at[my_k], ret_recv.at[c]
                 pltpu.make_async_remote_copy(
-                    src_ref=outgoing[c].at[dest], dst_ref=returned[c].at[my_k], send_sem=ret_send.at[c],
-                    recv_sem=ret_recv.at[c], device_id=(z, dest), device_id_type=MESH,
+                    src_ref=outgoing[c].at[dest], dst_ref=landing, send_sem=ret_send.at[c], recv_sem=sem,
+                    device_id=(shifted(z, my_t, lax.rem(dest, 2), 1) if c == 0 else z, dest), device_id_type=MESH,
                 ).start()
                 return carry
 
-            lax.fori_loop(1, DP, send, 0)
+            lax.fori_loop(0 if c == 0 else 1, DP, send, 0)
+
+    pltpu.make_async_copy(bouncing, bouncing, bounce_recv).wait()
+
+    def bounce(i, carry):
+        t = i // SIDE + 1
+        pltpu.make_async_remote_copy(
+            src_ref=bouncing.at[i], dst_ref=returned[0].at[lax.rem(i, SIDE) * (SIDE - 1) + t - 1], send_sem=bounce_send,
+            recv_sem=ret_recv.at[0], device_id=(shifted(z, t, core, -1), me), device_id_type=MESH,
+        ).start()
+        return carry
+
+    lax.fori_loop(0, MATS, bounce, 0)
 
     stores = []
-    for c, (start, width) in enumerate(SPREAD):
+    for c in (*range(1, len(SPREAD)), 0):
+        start, width = SPREAD[c]
         landing = returned[c]
 
-        @pl.when(is_owner)
-        def _():
-            others = landing.at[pl.ds(0, MATS - 1)]
-            pltpu.make_async_copy(others, others, ret_recv.at[c]).wait()
-
-        @pl.when(jnp.logical_not(is_owner))
-        def _():
+        if c == 0:
             pltpu.make_async_copy(landing, landing, ret_recv.at[c]).wait()
+        else:
+
+            @pl.when(is_owner)
+            def _():
+                others = landing.at[pl.ds(0, MATS - 1)]
+                pltpu.make_async_copy(others, others, ret_recv.at[c]).wait()
+
+            @pl.when(jnp.logical_not(is_owner))
+            def _():
+                pltpu.make_async_copy(landing, landing, ret_recv.at[c]).wait()
 
         def unpack_result(k, carry, landing=landing, start=start, half=width // 2):
             piece = landing[k].astype(F32)
@@ -318,11 +386,11 @@
         others = raw.at[pl.ds(0, 2 * (MATS - 1))]
         pltpu.make_async_copy(others, others, raw_send).wait()
         for c, buffer in enumerate(leads):
-            others = buffer.at[pl.ds(0, MATS - 1)]
-            pltpu.make_async_copy(others, others, lead_send.at[c]).wait()
+            sent = buffer.at[pl.ds(0, MATS if c == 0 else MATS - 1)]
+            pltpu.make_async_copy(sent, sent, lead_send.at[c]).wait()
         for c, buffer in enumerate(outgoing):
-            others = buffer.at[pl.ds(0, DP - 1)]
-            pltpu.make_async_copy(others, others, ret_send.at[c]).wait()
+            sent = buffer.at[pl.ds(0, DP if c == 0 else DP - 1)]
+            pltpu.make_async_copy(sent, sent, ret_send.at[c]).wait()
 
     @pl.when(jnp.logical_not(is_owner))
     def _():
@@ -330,6 +398,11 @@
         for c, buffer in enumerate(leads):
             pltpu.make_async_copy(buffer, buffer, lead_send.at[c]).wait()
 
+    @pl.when(my_t == 0)
+    def _():
+        pltpu.make_async_copy(passing, passing, pass_send).wait()
+
+    pltpu.make_async_copy(bouncing, bouncing, bounce_send).wait()
     store_nm.wait()
     for store in stores:
         store.wait()
@@ -363,6 +436,8 @@
             pltpu.VMEM(square, BF16),
             [pieces(DP, width) for _, width in SPREAD],
             [pieces(MATS, width) for _, width in SPREAD],
+            pltpu.VMEM((SIDE - 1, CHIPS, PIECE, NARROW // 2), BF16),
+            pieces(MATS, NARROW),
             pltpu.VMEM((SUM_PEERS, 8, 128), F32),
             pltpu.VMEM((SUM_PEERS, 8, 128), F32),
             pltpu.SemaphoreType.DMA((4,)),
@@ -376,6 +451,10 @@
             pltpu.SemaphoreType.DMA((len(GATHER) - 1,)),
             pltpu.SemaphoreType.DMA((len(SPREAD),)),
             pltpu.SemaphoreType.DMA((len(SPREAD),)),
+            pltpu.SemaphoreType.DMA,
+            pltpu.SemaphoreType.DMA((SIDE - 1,)),
+            pltpu.SemaphoreType.DMA,
+            pltpu.SemaphoreType.DMA,
         ],
         compiler_params=pltpu.CompilerParams(
             collective_id=0, has_side_effects=True, vmem_limit_bytes=51 * 1024 * 1024 + 256 * 1024

time: 66.4 us -> 63.9 us (0.962)
  Pallas kernels: 63.7 us -> 61.1 us
    pallas_call x1, Pallas kernels: 63.7 us -> 61.1 us  [shards(): pl.pallas_call(kernel, out_shape=(out, out), in_specs=[pl.BlockSpec(memor...]
where the time goes in v3:
time: 63.9 us; the launch traced here: 63.7 us
  Pallas kernels  61.1 us (96%)
  local copies, waits for them, and re-layouts  2.03 us (3%)
  between operations  0.64 us (1%)
    pallas_call x1, Pallas kernels, shards(): pl.pallas_call(kernel, out_shape=(out, out), in_specs=[pl.BlockSpec(memor...  61.1 us
    unnamed x2, local copies, waits for them, and re-layouts  2.03 us

profile of v3, /device:TPU:1, one launch (start us, length us, event | category | flops | bytes accessed | tf_op | source)
XLA Modules:
  0.0 63.7 jit_solution(14766000027771846430)
XLA Ops:
  0.6 61.1 %muon_step.1 = (bf16[12,24,2048]{2,1,0:T(8,128)(2,1)S(1)}, bf16[12,24,2048]{2,1,0:T(8,128)(2,1)S(1)}) custom-call(bf16[12,24,2048]{2,1,0:T(8,128)(2,1)} %bitcast.6, bf16[12,24,2048]{2,1,0:T(8,128)(2,1)} %bitcast.7), custom_call_target="tpu_custom_call" | custom-call | tf_op jit(solution)/shard_map/muon_step/pallas_call | solution.py:416
  61.7 1.0 %copy.6 = bf16[4,3,24,2048]{3,2,1,0:T(8,128)(2,1)} copy(bf16[4,3,24,2048]{3,2,1,0:T(8,128)(2,1)S(1)} %bitcast.5) | data formatting | bytes 2359296
  62.7 1.0 %copy.7 = bf16[4,3,24,2048]{3,2,1,0:T(8,128)(2,1)} copy(bf16[4,3,24,2048]{3,2,1,0:T(8,128)(2,1)S(1)} %bitcast.4) | data formatting | bytes 2359296

commit v4 on v3

--- a/solution.py
+++ b/solution.py
@@ -31,7 +31,8 @@
 PIECE = 2 * ROWS
 SUM_PEERS = 16
 GATHER = ((0, NARROW), (NARROW, NARROW), (512, COLS), (1024, COLS), (1536, COLS))
-SPREAD = ((0, NARROW), (512, COLS), (1024, COLS), (1536, COLS), (NARROW, NARROW))
+SPREAD = ((0, NARROW), (NARROW, NARROW), (512, COLS), (1024, COLS), (1536, COLS))
+AROUND = 1
 
 
 def hops(step, size):
@@ -96,7 +97,6 @@
         part = pl.ds(3 * k, 3)
         pltpu.make_async_copy(g_hbm.at[part], g_v.at[part], g_sem.at[k]).start()
     load_m = pltpu.make_async_copy(m_hbm, m_v, m_sem)
-    load_m.start()
 
     barrier = pltpu.get_barrier_semaphore()
     for i in range(1, SUM_PEERS):
@@ -121,6 +121,8 @@
             wide = wide[:, 0:256] + wide[:, 256:512]
             return carry + (wide[:, 0:128] + wide[:, 128:256])
 
+        if k == 3:
+            load_m.start()
         total = lax.fori_loop(12 * k, 12 * k + 12, squares, total, unroll=4)
 
     others_owning = jnp.where(my_t != 0, MATS - 1, MATS)
@@ -187,18 +189,18 @@
         ).start()
         return carry
 
-    lax.fori_loop(0, MATS, send_around, 0)
-
     for c in range(2, len(GATHER)):
         columns = pl.ds(*GATHER[c])
 
         def send_lead(i, carry, columns=columns, c=c):
+            if c == 2:
+                send_around(i, carry)
             k = lax.rem(i + me, MATS)
             piece = stack_halves(combine(g_v[k, :, columns], m_v[k, :, columns])[1]).astype(BF16)
             push(piece, leads[c - 1], k, recvs[c - 1], k, lead_send.at[c - 1], lead_recv.at[c - 1])
             return carry
 
-        lax.fori_loop(0, MATS, send_lead, 0)
+        lax.fori_loop(0, MATS, send_lead, 0, unroll=2)
 
     @pl.when(my_t == 0)
     def _():
@@ -319,41 +321,41 @@
                 rows = slice(d * ROWS, (d + 1) * ROWS)
                 outgoing[c][d] = jnp.concatenate([part[rows] for part in parts], axis=0).astype(BF16)
 
-            if c > 0:
+            if c != AROUND:
                 returned[c][my_k] = outgoing[c][me]
 
             def send(i, carry, c=c):
                 dest = lax.rem(me + i, DP)
-                if c == 0:
+                if c == AROUND:
                     landing, sem = bouncing.at[(my_t - 1) * SIDE + my_x], bounce_recv
                 else:
                     landing, sem = returned[c].at[my_k], ret_recv.at[c]
                 pltpu.make_async_remote_copy(
                     src_ref=outgoing[c].at[dest], dst_ref=landing, send_sem=ret_send.at[c], recv_sem=sem,
-                    device_id=(shifted(z, my_t, lax.rem(dest, 2), 1) if c == 0 else z, dest), device_id_type=MESH,
+                    device_id=(shifted(z, my_t, lax.rem(dest, 2), 1) if c == AROUND else z, dest), device_id_type=MESH,
                 ).start()
                 return carry
 
-            lax.fori_loop(0 if c == 0 else 1, DP, send, 0)
+            lax.fori_loop(0 if c == AROUND else 1, DP, send, 0, unroll=True)
 
     pltpu.make_async_copy(bouncing, bouncing, bounce_recv).wait()
 
     def bounce(i, carry):
         t = i // SIDE + 1
         pltpu.make_async_remote_copy(
-            src_ref=bouncing.at[i], dst_ref=returned[0].at[lax.rem(i, SIDE) * (SIDE - 1) + t - 1], send_sem=bounce_send,
-            recv_sem=ret_recv.at[0], device_id=(shifted(z, t, core, -1), me), device_id_type=MESH,
+            src_ref=bouncing.at[i], dst_ref=returned[AROUND].at[lax.rem(i, SIDE) * (SIDE - 1) + t - 1], send_sem=bounce_send,
+            recv_sem=ret_recv.at[AROUND], device_id=(shifted(z, t, core, -1), me), device_id_type=MESH,
         ).start()
         return carry
 
     lax.fori_loop(0, MATS, bounce, 0)
 
     stores = []
-    for c in (*range(1, len(SPREAD)), 0):
+    for c in sorted(range(len(SPREAD)), key=lambda c: c == AROUND):
         start, width = SPREAD[c]
         landing = returned[c]
 
-        if c == 0:
+        if c == AROUND:
             pltpu.make_async_copy(landing, landing, ret_recv.at[c]).wait()
         else:
 
@@ -389,7 +391,7 @@
             sent = buffer.at[pl.ds(0, MATS if c == 0 else MATS - 1)]
             pltpu.make_async_copy(sent, sent, lead_send.at[c]).wait()
         for c, buffer in enumerate(outgoing):
-            sent = buffer.at[pl.ds(0, DP if c == 0 else DP - 1)]
+            sent = buffer.at[pl.ds(0, DP if c == AROUND else DP - 1)]
             pltpu.make_async_copy(sent, sent, ret_send.at[c]).wait()
 
     @pl.when(jnp.logical_not(is_owner))

time: 63.9 us -> 61.9 us (0.969)
  Pallas kernels: 61.1 us -> 59.1 us
    pallas_call x1, Pallas kernels: 61.1 us -> 59.1 us  [shards(): pl.pallas_call(kernel, out_shape=(out, out), in_specs=[pl.BlockSpec(memor...]
where the time goes in v4:
time: 61.9 us; the launch traced here: 61.7 us
  Pallas kernels  59.1 us (95%)
  local copies, waits for them, and re-layouts  2.03 us (3%)
  between operations  0.64 us (1%)
    pallas_call x1, Pallas kernels, shards(): pl.pallas_call(kernel, out_shape=(out, out), in_specs=[pl.BlockSpec(memor...  59.1 us
    unnamed x2, local copies, waits for them, and re-layouts  2.03 us

profile of v4, /device:TPU:1, one launch (start us, length us, event | category | flops | bytes accessed | tf_op | source)
XLA Modules:
  0.0 61.7 jit_solution(15980610190473497616)
XLA Ops:
  0.6 59.1 %muon_step.1 = (bf16[12,24,2048]{2,1,0:T(8,128)(2,1)S(1)}, bf16[12,24,2048]{2,1,0:T(8,128)(2,1)S(1)}) custom-call(bf16[12,24,2048]{2,1,0:T(8,128)(2,1)} %bitcast.6, bf16[12,24,2048]{2,1,0:T(8,128)(2,1)} %bitcast.7), custom_call_target="tpu_custom_call" | custom-call | tf_op jit(solution)/shard_map/muon_step/pallas_call | solution.py:418
  59.7 1.0 %copy.6 = bf16[4,3,24,2048]{3,2,1,0:T(8,128)(2,1)} copy(bf16[4,3,24,2048]{3,2,1,0:T(8,128)(2,1)S(1)} %bitcast.5) | data formatting | bytes 2359296
  60.7 1.0 %copy.7 = bf16[4,3,24,2048]{3,2,1,0:T(8,128)(2,1)} copy(bf16[4,3,24,2048]{3,2,1,0:T(8,128)(2,1)S(1)} %bitcast.4) | data formatting | bytes 2359296

commit v5 on v4

--- a/solution.py
+++ b/solution.py
@@ -313,10 +313,11 @@
         for c, (start, width) in enumerate(SPREAD):
             half = width // 2
             parts = []
-            for columns in (pl.ds(start, half), pl.ds(start + half, half)):
-                right = full[:, columns]
+            for first in range(start, start + width, 256):
+                right = full[:, pl.ds(first, 256)]
                 new = jnp.dot(prod[...], right, preferred_element_type=F32)
-                parts.append((new + lin_coef * lin_coef * right.astype(F32)) * scale)
+                new = (new + lin_coef * lin_coef * right.astype(F32)) * scale
+                parts.extend((new[:, :half], new[:, half:]) if half < 256 else (new,))
             for d in range(DP):
                 rows = slice(d * ROWS, (d + 1) * ROWS)
                 outgoing[c][d] = jnp.concatenate([part[rows] for part in parts], axis=0).astype(BF16)

time: 61.9 us -> 61.7 us (level)
  no operation moved by 1% of the time
where the time goes in v5:
time: 61.7 us; the launch traced here: 61.5 us
  Pallas kernels  58.9 us (95%)
  local copies, waits for them, and re-layouts  2.03 us (3%)
  between operations  0.64 us (1%)
    pallas_call x1, Pallas kernels, shards(): pl.pallas_call(kernel, out_shape=(out, out), in_specs=[pl.BlockSpec(memor...  58.9 us
    unnamed x2, local copies, waits for them, and re-layouts  2.03 us

profile of v5, /device:TPU:1, one launch (start us, length us, event | category | flops | bytes accessed | tf_op | source)
XLA Modules:
  0.0 61.5 jit_solution(8773416557096166342)
XLA Ops:
  0.6 58.9 %muon_step.1 = (bf16[12,24,2048]{2,1,0:T(8,128)(2,1)S(1)}, bf16[12,24,2048]{2,1,0:T(8,128)(2,1)S(1)}) custom-call(bf16[12,24,2048]{2,1,0:T(8,128)(2,1)} %bitcast.6, bf16[12,24,2048]{2,1,0:T(8,128)(2,1)} %bitcast.7), custom_call_target="tpu_custom_call" | custom-call | tf_op jit(solution)/shard_map/muon_step/pallas_call | solution.py:419
  59.5 1.0 %copy.6 = bf16[4,3,24,2048]{3,2,1,0:T(8,128)(2,1)} copy(bf16[4,3,24,2048]{3,2,1,0:T(8,128)(2,1)S(1)} %bitcast.5) | data formatting | bytes 2359296
  60.5 1.0 %copy.7 = bf16[4,3,24,2048]{3,2,1,0:T(8,128)(2,1)} copy(bf16[4,3,24,2048]{3,2,1,0:T(8,128)(2,1)S(1)} %bitcast.4) | data formatting | bytes 2359296
